TPU v7x, 256 devices: a whole 4x4x8 slice. The times are simulated.
256 devices in a mesh: dp: 32 (over x, z), ctx: 8 (over y, core).
Axes of the slice: x: 4, y: 4, z: 8, core: 2. Of those that a mesh axis runs over, the one named last changes fastest.
Arguments:
- queries: bfloat16 [128, 512, 2048], P('dp', 'ctx'), may hold values from -72 to 72
- keyvals: bfloat16 [128, 512, 1024], P('dp', 'ctx'), may hold values from -6 to 6
- segments: int32 [128, 512], replicated, may hold values from 0 to 3, never falling along the last dimension, each value on 1 to 256 neighbouring positions
- plan: int32 [128], replicated, may hold values from 0 to 127, as said below
Outputs:
- attended: bfloat16 [128, 512, 2048], P('dp', 'ctx')
Inputs may be any that keep to these rules, and one draw needn't show every extreme that they name: plan is a permutation; every data rank receives 4 packs, no data rank sends more than 1 packs to one data rank, and some pairs of ranks reach that.
All inputs are finite; a program needn't handle non-finite values.
Results may differ from a plain program's by a relative error of at most 0.01.
Values may be sent and summed in bfloat16 or wider, within the bound.
A program may use at most 64 MiB of HBM per device.

v0:
```python
import jax
import jax.numpy as jnp
from jax import lax
from jax.sharding import PartitionSpec as P

HEAD_DIM = 64


def for_sending(value):

    def short(part):
        return part.astype(jnp.bfloat16) if part.dtype == jnp.float32 else part

    return jax.tree.map(short, value)


def attend_pack(q_pack, kv_pack, seg_pack):
    length = q_pack.shape[0]
    kv_count = kv_pack.shape[1] // (2 * HEAD_DIM)
    group_size = q_pack.shape[1] // (HEAD_DIM * kv_count)
    q_heads = q_pack.reshape(length, kv_count, group_size, HEAD_DIM)
    kv_heads = kv_pack.reshape(length, kv_count, 2, HEAD_DIM)
    pos_ids = jnp.arange(length, dtype=jnp.int32)
    block = min(512, length)
    scores = jnp.einsum(
        "qhgd,khd->hgqk", q_heads, kv_heads[:block, :, 0], preferred_element_type=jnp.float32
    ) * HEAD_DIM ** (-0.5)
    allowed = (seg_pack[0:block, None] == seg_pack[None, :block]) & (
        pos_ids[None, :block] <= pos_ids[0:block, None]
    )
    scores = jnp.where(allowed, scores, jnp.float32(-1e30))
    row_max = jnp.max(scores, axis=-1, keepdims=True)
    exp_sc = jnp.exp(scores - row_max)
    weights = (exp_sc / jnp.sum(exp_sc, axis=-1, keepdims=True)).astype(jnp.bfloat16)
    mixed_out = jnp.einsum(
        "hgqk,khd->qhgd", weights, kv_heads[:block, :, 1], preferred_element_type=jnp.float32
    )
    pieces = [mixed_out.astype(jnp.bfloat16).reshape(block, -1)]
    return jnp.concatenate(pieces, axis=0)


def attend_group(q_rows, kv_rows, seg_rows):
    q_heads, kv_heads = (
        lax.all_to_all(q_rows, "ctx", split_axis=2, concat_axis=1, tiled=True),
        lax.all_to_all(kv_rows, "ctx", split_axis=2, concat_axis=1, tiled=True),
    )

    def per_pack(inputs):
        return attend_pack(inputs[0], inputs[1], inputs[2])

    finished = lax.map(per_pack, (q_heads, kv_heads, seg_rows))
    return jax.tree.map(
        lambda part, own: part.astype(own.dtype),
        lax.all_to_all(for_sending(finished), "ctx", split_axis=1, concat_axis=2, tiled=True),
        finished,
    )


def send_table(plan, self_rank, pack_count, rank_count, slot_depth):
    dest_rank = lax.dynamic_slice_in_dim(plan, self_rank * pack_count, pack_count) // pack_count
    slot_order = jnp.arange(pack_count, dtype=jnp.int32)
    earlier = jnp.sum(
        (
            (dest_rank[None, :] == dest_rank[:, None]) & (slot_order[None, :] < slot_order[:, None])
        ).astype(jnp.int32),
        axis=1,
    )
    slot_table = (
        jnp.full((rank_count * slot_depth,), pack_count, jnp.int32)
        .at[dest_rank * slot_depth + earlier]
        .set(slot_order)
    )
    return slot_table


def receive_table(plan, self_rank, pack_count, rank_count, slot_depth):
    pack_total = plan.shape[0]
    source = (
        jnp.zeros((pack_total,), jnp.int32).at[plan].set(jnp.arange(pack_total, dtype=jnp.int32))
    )
    wanted = lax.dynamic_slice_in_dim(source, self_rank * pack_count, pack_count)
    src_rank = wanted // pack_count
    local_slot = wanted % pack_count
    bound_here = (plan // pack_count == self_rank).astype(jnp.int32).reshape(rank_count, pack_count)
    ahead_count = jnp.cumsum(bound_here, axis=1) - bound_here
    return (src_rank * slot_depth + ahead_count[src_rank, local_slot], wanted)


def pick_rows(stack, slot_table):
    pack_count = stack.shape[0]
    is_valid = slot_table < pack_count
    safe_index = jnp.minimum(slot_table, pack_count - 1)
    taken_rows = jnp.take(stack, safe_index, axis=0)
    return jnp.where(is_valid[:, None, None], taken_rows, jnp.zeros_like(taken_rows))


def per_device(queries, keyvals, segments, plan):
    pack_count = queries.shape[0]
    rank_count = lax.axis_size("dp")
    slot_depth = max(1, pack_count // rank_count)
    self_rank = lax.axis_index("dp")
    slot_table = send_table(plan, self_rank, pack_count, rank_count, slot_depth)
    recv_index, wanted = receive_table(plan, self_rank, pack_count, rank_count, slot_depth)
    q_arrived, kv_arrived = (
        lax.all_to_all(
            pick_rows(queries, slot_table), "dp", split_axis=0, concat_axis=0, tiled=True
        ),
        lax.all_to_all(
            pick_rows(keyvals, slot_table), "dp", split_axis=0, concat_axis=0, tiled=True
        ),
    )
    moved_q = jnp.take(q_arrived, recv_index, axis=0)
    moved_kv = jnp.take(kv_arrived, recv_index, axis=0)
    moved_seg = jnp.take(segments, wanted, axis=0)
    return attend_group(moved_q, moved_kv, moved_seg)


def solution(mesh):
    return jax.shard_map(
        per_device,
        mesh=mesh,
        in_specs=(P("dp", "ctx", None), P("dp", "ctx", None), P(), P()),
        out_specs=P("dp", "ctx", None),
        check_vma=False,
    )
```

profile of v0, /device:TPU:1, one launch (start us, length us, event | category | flops | bytes accessed | tf_op | source)
XLA Modules:
  0.0 402.5 jit_solution(9606788350219884394)
XLA Ops:
  0.8 1.0 scatter_custom_fusion
  3.3 3.8 gather_fusion.1
  7.1 4.7 %select_select_fusion.1 = bf16[32,64,1024]{2,1,0:T(8,128)(2,1)} fusion(bf16[32,64,1024]{2,1,0:T(8,128)(2,1)} %gather_fusion.1, pred[32]{0:T(512)(128)(4,1)S(1)} %get-tuple-element.74, pred[32]{0:T(512)(128)(4,1)S(1)} %get-tuple-element.78), kind=kLoop, calls=%fused_computation.28 | loop fusion | flops 4194304 | bytes 8388672 | tf_op jit(solution)/shard_map/jit(_where)/select_n | solution.py:94
  11.8 12.0 %all-to-all-start = ((bf16[32,64,1024]{2,1,0:T(8,128)(2,1)}), bf16[32,64,1024]{2,1,0:T(8,128)(2,1)}, u32[]{:S(2)}, u32[]{:S(2)}) async-start(bf16[32,64,1024]{2,1,0:T(8,128)(2,1)} %select_select_fusion.1), calls=%async_computation | async-start | bytes 8388608 | tf_op jit(solution)/shard_map/all_to_all | solution.py:108
  23.8 4.8 %gather_fusion.4 = bf16[32,64,2048]{2,1,0:T(8,128)(2,1)} fusion(bf16[4,64,2048]{2,1,0:T(8,128)(2,1)S(1)} %copy-done, s32[1024]{0:T(1024)S(1)} %pad_clamp_fusion.2), kind=kCustom, calls=%fused_computation.4 | custom fusion | bytes 16777344 | tf_op jit(solution)/shard_map/jit(_take)/gather | solution.py:93
  28.5 7.6 %select_select_fusion = bf16[32,64,2048]{2,1,0:T(8,128)(2,1)} fusion(bf16[32,64,2048]{2,1,0:T(8,128)(2,1)} %gather_fusion.4, pred[32]{0:T(512)(128)(4,1)S(1)} %get-tuple-element.74, pred[32]{0:T(512)(128)(4,1)S(1)} %get-tuple-element.78), kind=kLoop, calls=%fused_computation.27 | loop fusion | flops 8388608 | bytes 16777280 | tf_op jit(solution)/shard_map/jit(_where)/select_n | solution.py:94
  36.1 80.4 %all-to-all-done = bf16[32,64,1024]{2,1,0:T(8,128)(2,1)} async-done(((bf16[32,64,1024]{2,1,0:T(8,128)(2,1)}), bf16[32,64,1024]{2,1,0:T(8,128)(2,1)}, u32[]{:S(2)}, u32[]{:S(2)}) %all-to-all-start) | async-done | bytes 4194336 | tf_op jit(solution)/shard_map/all_to_all | solution.py:108
  116.5 9.4 %all-to-all-start.2 = ((bf16[32,64,2048]{2,1,0:T(8,128)(2,1)}), bf16[32,64,2048]{2,1,0:T(8,128)(2,1)}, u32[]{:S(2)}, u32[]{:S(2)}) async-start(bf16[32,64,2048]{2,1,0:T(8,128)(2,1)} %select_select_fusion), calls=%async_computation.2 | async-start | bytes 16777216 | tf_op jit(solution)/shard_map/all_to_all | solution.py:105
  126.9 2.8 gather_fusion.2
  130.5 1.5 reshape.156
  132.0 177.8 %all-to-all-done.2 = bf16[32,64,2048]{2,1,0:T(8,128)(2,1)} async-done(((bf16[32,64,2048]{2,1,0:T(8,128)(2,1)}), bf16[32,64,2048]{2,1,0:T(8,128)(2,1)}, u32[]{:S(2)}, u32[]{:S(2)}) %all-to-all-start.2) | async-done | bytes 8388640 | tf_op jit(solution)/shard_map/all_to_all | solution.py:105
  309.8 10.0 %all-to-all-start.1 = ((bf16[8,2,16384]{2,1,0:T(2,128)(2,1)}), bf16[8,2,16384]{2,1,0:T(2,128)(2,1)}, u32[]{:S(2)}, u32[]{:S(2)}) async-start(bf16[8,2,16384]{2,1,0:T(2,128)(2,1)} %reshape.156), calls=%async_computation.1 | async-start | bytes 1048576 | tf_op jit(solution)/shard_map/all_to_all | solution.py:45
  319.8 4.0 gather_fusion.5
  323.8 1.1 broadcast_select_fusion
  324.9 2.9 copy.46
  327.8 2.7 reshape.158
  330.5 4.8 %all-to-all-start.3 = ((bf16[8,2,32768]{2,1,0:T(2,128)(2,1)}), bf16[8,2,32768]{2,1,0:T(2,128)(2,1)}, u32[]{:S(2)}, u32[]{:S(2)}) async-start(bf16[8,2,32768]{2,1,0:T(2,128)(2,1)} %reshape.158), calls=%async_computation.3 | async-start | bytes 2097152 | tf_op jit(solution)/shard_map/all_to_all | solution.py:44
  335.4 1.5 gather_fusion.3
  337.0 2.7 reshape.157
  339.7 1.3 copy.56
  341.0 9.4 %all-to-all-done.3 = bf16[8,2,32768]{2,1,0:T(2,128)(2,1)} async-done(((bf16[8,2,32768]{2,1,0:T(2,128)(2,1)}), bf16[8,2,32768]{2,1,0:T(2,128)(2,1)}, u32[]{:S(2)}, u32[]{:S(2)}) %all-to-all-start.3) | async-done | bytes 1048608 | tf_op jit(solution)/shard_map/all_to_all | solution.py:44
  350.5 3.1 reshape.159
  353.6 2.4 copy.58
  356.0 25.2 %while.10 = (s32[]{:T(128)}, bf16[4,512,256]{1,2,0:T(8,128)(2,1)}, bf16[4,512,128]{2,1,0:T(8,128)(2,1)}, s32[4,512]{1,0:T(4,128)S(1)}, bf16[4,512,256]{2,1,0:T(8,128)(2,1)}, /*index=5*/s32[]{:T(128)}) while((s32[]{:T(128)}, bf16[4,512,256]{1,2,0:T(8,128)(2,1)}, bf16[4,512,128]{2,1,0:T(8,128)(2,1)}, s32[4,512]{1,0:T(4,128)S(1)}, ...), condition=%wide.region_7.8_spmd, body=%wide.region_4.7_spmd.sunk | while | flops 281931776 | bytes 16431697 | solution.py:51
  357.2 1.0 constant_dynamic-slice_fusion.7
  360.2 1.4 fusion.33
  366.5 1.4 fusion.33
  372.8 1.4 fusion.33
  379.1 1.4 fusion.33
  381.2 1.7 copy.51
  382.9 18.4 %all_to_all.64 = bf16[4,512,256]{2,0,1:T(4,128)(2,1)S(1)} all-to-all(bf16[4,512,256]{2,0,1:T(4,128)(2,1)S(1)} %copy.51), channel_id=1, replica_groups=mesh['dp'=32,'ctx'=8] {'ctx'}, dimensions={1} | all-to-all | bytes 2097152 | tf_op jit(solution)/shard_map/all_to_all | solution.py:54
  401.4 1.1 copy.61
  (63 shorter events, 23.0 us)
Async XLA Ops:
  0.0 23.8 %copy-start = (bf16[4,64,2048]{2,1,0:T(8,128)(2,1)S(1)}, bf16[4,64,2048]{2,1,0:T(8,128)(2,1)}, u32[]{:S(2)}) copy-start(bf16[4,64,2048]{2,1,0:T(8,128)(2,1)} %param.6) | copy-start | bytes 3145732
  11.8 104.8 %all-to-all-start = ((bf16[32,64,1024]{2,1,0:T(8,128)(2,1)}), bf16[32,64,1024]{2,1,0:T(8,128)(2,1)}, u32[]{:S(2)}, u32[]{:S(2)}) async-start(bf16[32,64,1024]{2,1,0:T(8,128)(2,1)} %select_select_fusion.1), calls=%async_computation | async-start | bytes 8388608 | tf_op jit(solution)/shard_map/all_to_all | solution.py:108
  36.1 89.8 %copy-start.1 = (s32[128]{0:T(128)S(1)}, s32[128]{0:T(128)}, u32[]{:S(2)}) copy-start(s32[128]{0:T(128)} %param.9) | copy-start | bytes 1540
  116.5 193.2 %all-to-all-start.2 = ((bf16[32,64,2048]{2,1,0:T(8,128)(2,1)}), bf16[32,64,2048]{2,1,0:T(8,128)(2,1)}, u32[]{:S(2)}, u32[]{:S(2)}) async-start(bf16[32,64,2048]{2,1,0:T(8,128)(2,1)} %select_select_fusion), calls=%async_computation.2 | async-start | bytes 16777216 | tf_op jit(solution)/shard_map/all_to_all | solution.py:105
  309.8 20.7 %all-to-all-start.1 = ((bf16[8,2,16384]{2,1,0:T(2,128)(2,1)}), bf16[8,2,16384]{2,1,0:T(2,128)(2,1)}, u32[]{:S(2)}, u32[]{:S(2)}) async-start(bf16[8,2,16384]{2,1,0:T(2,128)(2,1)} %reshape.156), calls=%async_computation.1 | async-start | bytes 1048576 | tf_op jit(solution)/shard_map/all_to_all | solution.py:45
  330.5 20.0 %all-to-all-start.3 = ((bf16[8,2,32768]{2,1,0:T(2,128)(2,1)}), bf16[8,2,32768]{2,1,0:T(2,128)(2,1)}, u32[]{:S(2)}, u32[]{:S(2)}) async-start(bf16[8,2,32768]{2,1,0:T(2,128)(2,1)} %reshape.158), calls=%async_computation.3 | async-start | bytes 2097152 | tf_op jit(solution)/shard_map/all_to_all | solution.py:44
where the time goes:
time: 410 us; the launch traced here: 402 us
  waiting for transfers between devices  268 us (65%)
  local copies, waits for them, and re-layouts  50.9 us (12%)
  starting transfers between devices  36.2 us (9%)
  other arithmetic  20 us (5%)
  blocking collectives  18.4 us (4%)
  matrix products  9.1 us (2%)
    all_to_all x1, waiting for transfers between devices, per_device(): lax.all_to_all(pick_rows(queries, slot_table), 'dp', split_axis=0, concat...  178 us
    all_to_all x1, waiting for transfers between devices, per_device(): lax.all_to_all(pick_rows(keyvals, slot_table), 'dp', split_axis=0, concat...  80.4 us
    all_to_all x1, blocking collectives, attend_group(): lax.all_to_all(for_sending(finished), 'ctx', split_axis=1, concat_axis=2,...  18.4 us
    select_n x2, other arithmetic, pick_rows(): jnp.where(is_valid[:, None, None], taken_rows, jnp.zeros_like(taken_rows))  12.2 us
    all_to_all x1, starting transfers between devices, per_device(): lax.all_to_all(pick_rows(keyvals, slot_table), 'dp', split_axis=0, concat...  12 us
    all_to_all x1, starting transfers between devices, attend_group(): lax.all_to_all(kv_rows, 'ctx', split_axis=2, concat_axis=1, tiled=True)  10 us
    unnamed x8, local copies, waits for them, and re-layouts  9.98 us
    all_to_all x1, waiting for transfers between devices, attend_group(): lax.all_to_all(q_rows, 'ctx', split_axis=2, concat_axis=1, tiled=True)  9.45 us
  transfers between devices with their start and end apart: 4, of which 3 were waited for; matrix products, arithmetic and copies ran while one was open for 9% of the time, Pallas kernels for 0%

commit v1 on v0

v1 whole, which is shorter than its diff:
```python
import functools

import jax
import jax.numpy as jnp
from jax import lax
from jax.experimental import pallas as pl
from jax.experimental.pallas import tpu as pltpu
from jax.sharding import PartitionSpec as P

MESH = pl.DeviceIdType.MESH
HEAD = 64
PACK = 512
PACKS = 4
ALL = 128
XN, ZN, CTX = 4, 8, 8
RANKS = XN * ZN
ROWS = PACK // CTX
SUB = ROWS // XN
LANES = 128
QB = 128
WINDOW = 384
NEG = -1e30
EXP2_SCALE = HEAD**-0.5 * 1.4426950408889634
NN = (((1,), (0,)), ((), ()))
NT = (((1,), (1,)), ((), ()))


def make_bias(seg_ref, row, bias, i):
    seg_row = seg_ref[pl.ds(row, 1), :]
    lower = lax.broadcasted_iota(jnp.int32, (QB, QB), 1) <= lax.broadcasted_iota(jnp.int32, (QB, QB), 0)
    for b in range(PACK // QB):
        seg_q = jnp.transpose(jnp.broadcast_to(seg_row[:, b * QB : (b + 1) * QB], (QB, QB)))
        first = max(0, b - 2)
        for kb in range(first, b + 1):
            seg_k = jnp.broadcast_to(seg_row[:, kb * QB : (kb + 1) * QB], (QB, QB))
            same = seg_q == seg_k
            if kb == b:
                same = same & lower
            bias[i, b * QB : (b + 1) * QB, (kb - first) * QB : (kb - first + 1) * QB] = jnp.where(same, 0.0, NEG)


def attend(q_c, kvf, bias, att_c, i):
    kv = kvf[i].astype(jnp.float32)
    swapped = pltpu.roll(kv, HEAD, 1)
    left = lax.broadcasted_iota(jnp.int32, (PACK, LANES), 1) < HEAD
    keys = (
        jnp.where(left, kv, 0.0).astype(jnp.bfloat16),
        jnp.where(left, 0.0, swapped).astype(jnp.bfloat16),
    )
    values = (
        jnp.where(left, swapped, 1.0).astype(jnp.bfloat16),
        jnp.where(left, 1.0, kv).astype(jnp.bfloat16),
    )
    left_q = lax.broadcasted_iota(jnp.int32, (QB, LANES), 1) < HEAD
    for b in range(PACK // QB):
        lo, hi = max(0, b - 2) * QB, (b + 1) * QB
        q = q_c[i, b * QB : hi, :]
        mask = bias[i, b * QB : hi, 0 : hi - lo]
        sums = []
        for h in range(2):
            s = lax.dot_general(q, keys[h][lo:hi], NT, preferred_element_type=jnp.float32) + mask
            top = jnp.max(s, axis=1, keepdims=True)
            p = jnp.exp2((s - top) * EXP2_SCALE).astype(jnp.bfloat16)
            sums.append(lax.dot_general(p, values[h][lo:hi], NN, preferred_element_type=jnp.float32))
        total = jnp.where(left_q, sums[0], sums[1])
        norm = pltpu.roll(jnp.where(left_q, sums[1], sums[0]), HEAD, 1)
        att_c[i, b * QB : hi, :] = (total / norm).astype(jnp.bfloat16)


def kernel(
    inv_ref, seg_ref, q_ref, kv_ref, out_ref,
    kvf, bias, qf0, qf1, att0, att1, mid0, mid1, snd0, snd1,
    kv_recv, q_recv, p1_send, mid_recv, mid_send, out_recv, out_send,
):
    rank, ctx = lax.axis_index("dp"), lax.axis_index("ctx")
    xs, zs = rank // ZN, rank % ZN
    qf, att, mid, snd = (qf0, qf1), (att0, att1), (mid0, mid1), (snd0, snd1)
    my_rows = pl.ds(pl.multiple_of(ctx * ROWS, ROWS), ROWS)

    def kv_cols(i, g):
        return kv_ref.at[i, :, pl.ds(pl.multiple_of(g * LANES, LANES), LANES)]

    def q_cols(i, g, c):
        return q_ref.at[i, :, pl.ds(pl.multiple_of(g * 2 * LANES + c * LANES, LANES), LANES)]

    def remote(src, dst, send, recv, to):
        pltpu.make_async_remote_copy(
            src_ref=src, dst_ref=dst, send_sem=send, recv_sem=recv, device_id=to, device_id_type=MESH
        ).start()

    def await_bytes(ref, sem):
        pltpu.make_async_copy(ref, ref, sem).wait()

    def give_kv_q0(n, _):
        i, g = n // (CTX - 1), (ctx + 1 + n % (CTX - 1)) % CTX
        remote(kv_cols(i, g), kvf.at[i, my_rows], p1_send.at[0], kv_recv.at[i], (rank, g))
        remote(q_cols(i, g, 0), qf0.at[i, my_rows], p1_send.at[1], q_recv.at[0, i], (rank, g))
        return 0

    def give_q1(n, _):
        i, g = n // (CTX - 1), (ctx + 1 + n % (CTX - 1)) % CTX
        remote(q_cols(i, g, 1), qf1.at[i, my_rows], p1_send.at[2], q_recv.at[1, i], (rank, g))
        return 0

    for i in range(PACKS):
        pltpu.make_async_copy(kv_cols(i, ctx), kvf.at[i, my_rows], kv_recv.at[i]).start()
        for c in range(2):
            pltpu.make_async_copy(q_cols(i, ctx, c), qf[c].at[i, my_rows], q_recv.at[c, i]).start()
    lax.fori_loop(0, PACKS * (CTX - 1), give_kv_q0, 0)
    lax.fori_loop(0, PACKS * (CTX - 1), give_q1, 0)

    def spread(c):
        def one(n, _):
            x, t = (xs + n // CTX) % XN, (ctx + n % CTX) % CTX
            to = x * ZN + (ctx + t) % ZN
            here = (to == rank) & (t == ctx)
            src = att[c].at[:, pl.ds(pl.multiple_of(t * ROWS + x * SUB, SUB), SUB), :]
            dst = mid[c].at[pl.ds(rank * PACKS, PACKS)]

            @pl.when(here)
            def _():
                pltpu.make_async_copy(src, dst, mid_recv.at[c]).start()

            @pl.when(jnp.logical_not(here))
            def _():
                remote(src, dst, mid_send.at[c], mid_recv.at[c], (to, t))

            return 0

        lax.fori_loop(0, RANKS, one, 0)

    for c in range(2):

        def work(i, _):
            if c == 0:
                await_bytes(kvf.at[i], kv_recv.at[i])
                make_bias(seg_ref, rank * PACKS + i, bias, i)
            await_bytes(qf[c].at[i], q_recv.at[c, i])
            attend(qf[c], kvf, bias, att[c], i)
            return 0

        lax.fori_loop(0, PACKS, work, 0)
        spread(c)

    head = (zs - ctx + ZN) % ZN

    for c in range(2):
        await_bytes(mid[c], mid_recv.at[c])

        def deliver(n, _):
            to = (xs + n // ZN) % XN * ZN + (zs + n % ZN) % ZN
            for j in range(PACKS):
                snd[c][to * PACKS + j] = mid[c][inv_ref[to * PACKS + j]]
            src = snd[c].at[pl.ds(to * PACKS, PACKS)]
            dst = out_ref.at[
                :,
                pl.ds(pl.multiple_of(xs * SUB, SUB), SUB),
                pl.ds(pl.multiple_of(head * 2 * LANES + c * LANES, LANES), LANES),
            ]

            @pl.when(to == rank)
            def _():
                pltpu.make_async_copy(src, dst, out_recv).start()

            @pl.when(to != rank)
            def _():
                remote(src, dst, out_send.at[c], out_recv, (to, ctx))

            return 0

        lax.fori_loop(0, RANKS, deliver, 0)

    await_bytes(kvf.at[:, 0 : PACK - ROWS], p1_send.at[0])
    await_bytes(qf0.at[:, 0 : PACK - ROWS], p1_send.at[1])
    await_bytes(qf1.at[:, 0 : PACK - ROWS], p1_send.at[2])
    keeps_one = (2 * ctx) % ZN == zs
    for c in range(2):

        @pl.when(keeps_one)
        def _():
            await_bytes(mid[c].at[0 : ALL - PACKS], mid_send.at[c])

        @pl.when(jnp.logical_not(keeps_one))
        def _():
            await_bytes(mid[c], mid_send.at[c])

        await_bytes(snd[c].at[0 : ALL - PACKS], out_send.at[c])
    await_bytes(out_ref, out_recv)


def per_device(queries, keyvals, segments, plan):
    order = jnp.arange(ALL, dtype=jnp.int32)
    inverse = jnp.sum(jnp.where(plan[:, None] == order[None, :], order[:, None], 0), axis=0)
    full = (PACKS, PACK, LANES)
    pieces = (ALL, SUB, LANES)
    dma = pltpu.SemaphoreType.DMA
    return pl.pallas_call(
        kernel,
        out_shape=jax.ShapeDtypeStruct((PACKS, ROWS, queries.shape[2]), jnp.bfloat16),
        in_specs=[
            pl.BlockSpec(memory_space=pltpu.SMEM),
            pl.BlockSpec(memory_space=pltpu.VMEM),
            pl.BlockSpec(memory_space=pl.ANY),
            pl.BlockSpec(memory_space=pl.ANY),
        ],
        out_specs=pl.BlockSpec(memory_space=pl.ANY),
        scratch_shapes=[
            pltpu.VMEM(full, jnp.bfloat16),
            pltpu.VMEM((PACKS, PACK, WINDOW), jnp.float32),
            *[pltpu.VMEM(full, jnp.bfloat16)] * 4,
            *[pltpu.VMEM(pieces, jnp.bfloat16)] * 4,
            dma((PACKS,)),
            dma((2, PACKS)),
            dma((3,)),
            dma((2,)),
            dma((2,)),
            dma(()),
            dma((2,)),
        ],
        compiler_params=pltpu.CompilerParams(has_side_effects=True, vmem_limit_bytes=24 * 2**20),
        cost_estimate=pl.CostEstimate(flops=2 * 10**9, bytes_accessed=4 * 2**20, transcendentals=2 * 10**6),
    )(inverse, segments, queries, keyvals)


def solution(mesh):
    return jax.shard_map(
        per_device,
        mesh=mesh,
        in_specs=(P("dp", "ctx", None), P("dp", "ctx", None), P(), P()),
        out_specs=P("dp", "ctx", None),
        check_vma=False,
    )
```

time: 410 us -> 103 us (0.25); the launches traced: 402 us -> 103 us
  waiting for transfers between devices: 268 us -> 0 us
  Pallas kernels: 0 us -> 97.8 us
  local copies, waits for them, and re-layouts: 50.9 us -> 4.18 us
  starting transfers between devices: 36.2 us -> 0 us
  other arithmetic: 20 us -> 0.75 us
  blocking collectives: 18.4 us -> 0 us
  matrix products: 9.1 us -> 0 us
    all_to_all x4 -> x0, waiting for transfers between devices: 268 us -> none  [the longest x1 178 us: per_device(): lax.all_to_all(pick_rows(queries, slot_table), 'dp', split_axis=0, concat...]
    pallas_call x0 -> x1, Pallas kernels: none -> 97.8 us  [per_device(): pl.pallas_call(kernel, out_shape=jax.ShapeDtypeStruct((PACKS, ROWS, queri...]
    all_to_all x4 -> x0, starting transfers between devices: 36.2 us -> none  [the longest x1 12 us: per_device(): lax.all_to_all(pick_rows(keyvals, slot_table), 'dp', split_axis=0, concat...]
    all_to_all x1 -> x0, blocking collectives: 18.4 us -> none  [attend_group(): lax.all_to_all(for_sending(finished), 'ctx', split_axis=1, concat_axis=2,...]
    gather x6 -> x0, local copies, waits for them, and re-layouts: 17.5 us -> none  [the longest x2 8.56 us: pick_rows(): taken_rows = jnp.take(stack, safe_index, axis=0)]
    select_n x7 -> x0, other arithmetic: 14.3 us -> none  [the longest x2 12.2 us: pick_rows(): jnp.where(is_valid[:, None, None], taken_rows, jnp.zeros_like(taken_rows))]
    dot_general x8 -> x0, matrix products: 9.1 us -> none  [the longest x4 5.52 us: attend_pack(): jnp.einsum('hgqk,khd->qhgd', weights, kv_heads[:block, :, 1], preferred_e...]
    dynamic_slice x20 -> x0, local copies, waits for them, and re-layouts: 8.62 us -> none  [attend_group(): finished = lax.map(per_pack, (q_heads, kv_heads, seg_rows))]
  transfers between devices with their start and end apart: 4 -> 0, of which waited for: 3 -> 0; matrix products, arithmetic and copies ran while one was open for 9% -> 0% of each run, Pallas kernels for 0% -> 0%
where the time goes in v1:
time: 103 us
  Pallas kernels  97.8 us (95%)
  local copies, waits for them, and re-layouts  4.18 us (4%)
    pallas_call x1, Pallas kernels, per_device(): pl.pallas_call(kernel, out_shape=jax.ShapeDtypeStruct((PACKS, ROWS, queri...  97.8 us
    unnamed x7, local copies, waits for them, and re-layouts  4.18 us

profile of v1, /device:TPU:1, one launch (start us, length us, event | category | flops | bytes accessed | tf_op | source)
XLA Modules:
  0.0 102.7 jit_solution(13803674379880923997)
XLA Ops:
  0.0 0.8 select_reduce_fusion.inv_ref
  0.8 0.0 copy-start
  0.8 1.2 %copy-done = bf16[4,64,2048]{2,1,0:T(8,128)(2,1)S(1)} copy-done((bf16[4,64,2048]{2,1,0:T(8,128)(2,1)S(1)}, bf16[4,64,2048]{2,1,0:T(8,128)(2,1)}, u32[]{:S(2)}) %copy-start) | copy-done | bytes 1048600
  2.0 0.0 copy-start.1
  2.0 1.0 %copy-done.1 = bf16[4,64,1024]{2,1,0:T(8,128)(2,1)S(1)} copy-done((bf16[4,64,1024]{2,1,0:T(8,128)(2,1)S(1)}, bf16[4,64,1024]{2,1,0:T(8,128)(2,1)}, u32[]{:S(2)}) %copy-start.1) | copy-done | bytes 524312
  3.0 0.0 copy-start.2
  3.0 0.9 copy-done.2
  4.0 97.8 %shard_map.46 = bf16[4,64,2048]{2,1,0:T(8,128)(2,1)S(1)} custom-call(s32[128]{0:T(128)S(1)} %select_reduce_fusion.inv_ref, s32[128,512]{1,0:T(8,128)S(1)} %copy-done.2, bf16[4,64,2048]{2,1,0:T(8,128)(2,1)S(1)} %copy-done, bf16[4,64,1024]{2,1,0:T(8,128)(2,1)S(1)} %copy-done.1), custom_call_target="tpu_custom_call" | custom-call | flops 2000000000 | bytes 4194304 | tf_op jit(solution)/shard_map/pallas_call | solution.py:197
  101.7 1.0 copy.6
Async XLA Ops:
  0.8 1.2 %copy-start = (bf16[4,64,2048]{2,1,0:T(8,128)(2,1)S(1)}, bf16[4,64,2048]{2,1,0:T(8,128)(2,1)}, u32[]{:S(2)}) copy-start(bf16[4,64,2048]{2,1,0:T(8,128)(2,1)} %q_ref.1) | copy-start | bytes 3145732
  2.0 1.0 %copy-start.1 = (bf16[4,64,1024]{2,1,0:T(8,128)(2,1)S(1)}, bf16[4,64,1024]{2,1,0:T(8,128)(2,1)}, u32[]{:S(2)}) copy-start(bf16[4,64,1024]{2,1,0:T(8,128)(2,1)} %kv_ref.1) | copy-start | bytes 1572868
  3.0 0.9 copy-start.2

commit v2 on v1

v2 whole, which is shorter than its diff:
```python
import functools

import jax
import jax.numpy as jnp
from jax import lax
from jax.experimental import pallas as pl
from jax.experimental.pallas import tpu as pltpu
from jax.sharding import PartitionSpec as P

MESH = pl.DeviceIdType.MESH
HEAD = 64
PACK = 512
PACKS = 4
ALL = 128
XN, ZN, CTX = 4, 8, 8
RANKS = XN * ZN
AHEAD = 4
ROWS = PACK // CTX
SUB = ROWS // XN
LANES = 128
QB = 128
WINDOW = 384
NEG = -1e30
EXP2_SCALE = HEAD**-0.5 * 1.4426950408889634
NN = (((1,), (0,)), ((), ()))
NT = (((1,), (1,)), ((), ()))


def make_bias(seg_ref, row, bias, i):
    seg_row = seg_ref[pl.ds(row, 1), :]
    lower = lax.broadcasted_iota(jnp.int32, (QB, QB), 1) <= lax.broadcasted_iota(jnp.int32, (QB, QB), 0)
    for b in range(PACK // QB):
        seg_q = jnp.transpose(jnp.broadcast_to(seg_row[:, b * QB : (b + 1) * QB], (QB, QB)))
        first = max(0, b - 2)
        for kb in range(first, b + 1):
            seg_k = jnp.broadcast_to(seg_row[:, kb * QB : (kb + 1) * QB], (QB, QB))
            same = seg_q == seg_k
            if kb == b:
                same = same & lower
            bias[i, b * QB : (b + 1) * QB, (kb - first) * QB : (kb - first + 1) * QB] = jnp.where(same, 0.0, NEG)


def attend(q_c, kvf, bias, att_c, i):
    kv = kvf[i].astype(jnp.float32)
    swapped = pltpu.roll(kv, HEAD, 1)
    left = lax.broadcasted_iota(jnp.int32, (PACK, LANES), 1) < HEAD
    keys = (
        jnp.where(left, kv, 0.0).astype(jnp.bfloat16),
        jnp.where(left, 0.0, swapped).astype(jnp.bfloat16),
    )
    values = (
        jnp.where(left, swapped, 1.0).astype(jnp.bfloat16),
        jnp.where(left, 1.0, kv).astype(jnp.bfloat16),
    )
    left_q = lax.broadcasted_iota(jnp.int32, (QB, LANES), 1) < HEAD
    for b in range(PACK // QB):
        lo, hi = max(0, b - 2) * QB, (b + 1) * QB
        q = q_c[i, b * QB : hi, :]
        mask = bias[i, b * QB : hi, 0 : hi - lo]
        sums = []
        for h in range(2):
            s = lax.dot_general(q, keys[h][lo:hi], NT, preferred_element_type=jnp.float32) + mask
            top = jnp.max(s, axis=1, keepdims=True)
            p = jnp.exp2((s - top) * EXP2_SCALE).astype(jnp.bfloat16)
            sums.append(lax.dot_general(p, values[h][lo:hi], NN, preferred_element_type=jnp.float32))
        total = jnp.where(left_q, sums[0], sums[1])
        norm = pltpu.roll(jnp.where(left_q, sums[1], sums[0]), HEAD, 1)
        att_c[i, b * QB : hi, :] = (total / norm).astype(jnp.bfloat16)


def kernel(
    plan_ref, seg_ref, q_ref, kv_ref, out_ref,
    kvf, bias, qf0, qf1, att0, att1, mid0, mid1, snd0, snd1, segs, inv_row, inv_ref, q_v, kv_v,
    kv_recv, q_recv, p1_send, mid_recv, mid_send, out_recv, out_send, small, group_in, all_in,
):
    rank, ctx = lax.axis_index("dp"), lax.axis_index("ctx")
    xs, zs = rank >> 3, rank & 7
    qf, att, mid, snd = (qf0, qf1), (att0, att1), (mid0, mid1), (snd0, snd1)
    my_rows = pl.ds(pl.multiple_of(ctx * ROWS, ROWS), ROWS)

    def kv_cols(i, g):
        return kv_v.at[i, :, pl.ds(pl.multiple_of(g * LANES, LANES), LANES)]

    def q_cols(i, g, c):
        return q_v.at[i, :, pl.ds(pl.multiple_of(g * 2 * LANES + c * LANES, LANES), LANES)]

    def remote(src, dst, send, recv, to):
        pltpu.make_async_remote_copy(
            src_ref=src, dst_ref=dst, send_sem=send, recv_sem=recv, device_id=to, device_id_type=MESH
        ).start()

    def await_bytes(ref, sem):
        pltpu.make_async_copy(ref, ref, sem).wait()

    def tell(sem, to):
        pl.semaphore_signal(sem, inc=1, device_id=to, device_id_type=MESH)

    def give_kv_q0(i):
        def one(n, _):
            g = (ctx + n) & 7
            remote(kv_cols(i, g), kvf.at[i, my_rows], p1_send.at[0], kv_recv.at[i], (rank, g))
            remote(q_cols(i, g, 0), qf0.at[i, my_rows], p1_send.at[1], q_recv.at[0, i], (rank, g))
            return 0

        for n in range(1, CTX):
            one(n, 0)

    def give_q1(i):
        def one(n, _):
            g = (ctx + n) & 7
            remote(q_cols(i, g, 1), qf1.at[i, my_rows], p1_send.at[2], q_recv.at[1, i], (rank, g))
            return 0

        for n in range(1, CTX):
            one(n, 0)

    barrier = pltpu.get_barrier_semaphore()

    @pl.when(ctx != 0)
    def _():
        tell(barrier, (rank, 0))

    first = pl.multiple_of((rank >> 1) * 2 * PACKS, 2 * PACKS)
    seg_copy = pltpu.make_async_copy(seg_ref.at[pl.ds(first, 2 * PACKS)], segs, small.at[0])
    seg_copy.start()
    own = (pltpu.make_async_copy(kv_ref, kv_v, small.at[2]), pltpu.make_async_copy(q_ref, q_v, small.at[3]))
    for copy in own:
        copy.start()

    @pl.when(ctx == 0)
    def _():
        pl.semaphore_wait(barrier, CTX - 1)
        lax.fori_loop(1, CTX, lambda m, _: (tell(group_in, (rank, m)), 0)[1], 0)

    @pl.when(ctx != 0)
    def _():
        pl.semaphore_wait(group_in, 1)

    for copy in own:
        copy.wait()
    for i in range(AHEAD):
        give_kv_q0(i)
    for i in range(PACKS):
        pltpu.make_async_copy(kv_cols(i, ctx), kvf.at[i, my_rows], kv_recv.at[i]).start()
        for c in range(2):
            pltpu.make_async_copy(q_cols(i, ctx, c), qf[c].at[i, my_rows], q_recv.at[c, i]).start()

    @pl.when(ctx == 0)
    def _():
        lax.fori_loop(0, RANKS, lambda m, _: (tell(barrier, ((rank + m) & 31, 1)), 0)[1], 0)


    place = jnp.transpose(jnp.broadcast_to(plan_ref[...], (ALL, ALL)))
    wanted = lax.broadcasted_iota(jnp.int32, (ALL, ALL), 1)
    source = lax.broadcasted_iota(jnp.int32, (ALL, ALL), 0)
    inv_row[...] = jnp.max(jnp.where(place == wanted, source, 0), axis=0, keepdims=True)
    inv_copy = pltpu.make_async_copy(inv_row, inv_ref, small.at[1])
    inv_copy.start()
    seg_copy.wait()

    @pl.when(ctx == 1)
    def _():
        pl.semaphore_wait(barrier, RANKS)
        lax.fori_loop(1, CTX, lambda m, _: (tell(all_in, (rank, (1 + m) & 7)), 0)[1], 0)

    def spread(c, i):
        dst = mid[c].at[rank * PACKS + i]

        def row(m, _):
            x = (xs + m) & 3
            for n in range(ZN):
                z = (zs + n) & 7
                block = ((z + ctx) & 7) * XN + x
                src = att[c].at[i, pl.ds(pl.multiple_of(block * SUB, SUB), SUB), :]
                if n:
                    remote(src, dst, mid_send.at[c], mid_recv.at[c], (x * ZN + z, ctx))
                else:

                    @pl.when(m == 0)
                    def _():
                        pltpu.make_async_copy(src, dst, mid_recv.at[c]).start()

                    @pl.when(m != 0)
                    def _():
                        remote(src, dst, mid_send.at[c], mid_recv.at[c], (x * ZN + z, ctx))

            return 0

        lax.fori_loop(0, XN, row, 0)

    for c in range(2):

        def work(i, _):
            if c == 0:
                await_bytes(kvf.at[i], kv_recv.at[i])
                make_bias(segs, (rank & 1) * PACKS + i, bias, i)
            await_bytes(qf[c].at[i], q_recv.at[c, i])
            attend(qf[c], kvf, bias, att[c], i)
            if c == 0:

                @pl.when((ctx != 1) & (i == 0))
                def _():
                    pl.semaphore_wait(all_in, 1)

            spread(c, i)
            later = i + AHEAD

            @pl.when(later < PACKS)
            def _():
                (give_kv_q0, give_q1)[c](later)

            if c == 0:

                @pl.when(later >= PACKS)
                def _():
                    give_q1(later - PACKS)

            return 0

        lax.fori_loop(0, PACKS, work, 0)

    inv_copy.wait()
    to_ctx = (zs + ctx) & 7

    for c in range(2):
        await_bytes(mid[c], mid_recv.at[c])

        dst = out_ref.at[
            :,
            pl.ds(pl.multiple_of(xs * SUB, SUB), SUB),
            pl.ds(pl.multiple_of(ctx * 2 * LANES + c * LANES, LANES), LANES),
        ]

        def deliver(m, _):
            for n in range(ZN):
                to = ((xs + m) & 3) * ZN + ((zs + n) & 7)
                for j in range(PACKS):
                    snd[c][to * PACKS + j] = mid[c][inv_ref[0, to * PACKS + j]]
                src = snd[c].at[pl.ds(to * PACKS, PACKS)]
                if n:
                    remote(src, dst, out_send.at[c], out_recv, (to, to_ctx))
                else:

                    here = (m == 0) & (zs == 0)

                    @pl.when(here)
                    def _():
                        pltpu.make_async_copy(src, dst, out_recv).start()

                    @pl.when(jnp.logical_not(here))
                    def _():
                        remote(src, dst, out_send.at[c], out_recv, (to, to_ctx))

            return 0

        lax.fori_loop(0, XN, deliver, 0)

    await_bytes(kvf.at[:, 0 : PACK - ROWS], p1_send.at[0])
    await_bytes(qf0.at[:, 0 : PACK - ROWS], p1_send.at[1])
    await_bytes(qf1.at[:, 0 : PACK - ROWS], p1_send.at[2])
    for c in range(2):
        await_bytes(mid[c].at[0 : ALL - PACKS], mid_send.at[c])

        @pl.when(zs == 0)
        def _():
            await_bytes(snd[c].at[0 : ALL - PACKS], out_send.at[c])

        @pl.when(zs != 0)
        def _():
            await_bytes(snd[c], out_send.at[c])

    await_bytes(out_ref, out_recv)


def per_device(queries, keyvals, segments, plan):
    full = (PACKS, PACK, LANES)
    pieces = (ALL, SUB, LANES)
    dma = pltpu.SemaphoreType.DMA
    return pl.pallas_call(
        kernel,
        out_shape=jax.ShapeDtypeStruct((PACKS, ROWS, queries.shape[2]), jnp.bfloat16),
        in_specs=[
            pl.BlockSpec(memory_space=pltpu.VMEM),
            pl.BlockSpec(memory_space=pl.ANY),
            pl.BlockSpec(memory_space=pl.ANY),
            pl.BlockSpec(memory_space=pl.ANY),
        ],
        out_specs=pl.BlockSpec(memory_space=pl.ANY),
        scratch_shapes=[
            pltpu.VMEM(full, jnp.bfloat16),
            pltpu.VMEM((PACKS, PACK, WINDOW), jnp.float32),
            *[pltpu.VMEM(full, jnp.bfloat16)] * 4,
            *[pltpu.VMEM(pieces, jnp.bfloat16)] * 4,
            pltpu.VMEM((2 * PACKS, PACK), jnp.int32),
            pltpu.VMEM((1, ALL), jnp.int32),
            pltpu.SMEM((1, ALL), jnp.int32),
            pltpu.VMEM(queries.shape, jnp.bfloat16),
            pltpu.VMEM(keyvals.shape, jnp.bfloat16),
            dma((PACKS,)),
            dma((2, PACKS)),
            dma((3,)),
            dma((2,)),
            dma((2,)),
            dma(()),
            dma((2,)),
            dma((4,)),
            pltpu.SemaphoreType.REGULAR,
            pltpu.SemaphoreType.REGULAR,
        ],
        compiler_params=pltpu.CompilerParams(collective_id=0, has_side_effects=True, vmem_limit_bytes=60 * 2**20),
        cost_estimate=pl.CostEstimate(flops=2 * 10**9, bytes_accessed=4 * 2**20, transcendentals=2 * 10**6),
    )(plan.reshape(1, ALL), segments, queries, keyvals)


def solution(mesh):
    return jax.shard_map(
        per_device,
        mesh=mesh,
        in_specs=(P("dp", "ctx", None), P("dp", "ctx", None), P(), P()),
        out_specs=P("dp", "ctx", None),
        check_vma=False,
    )
```

time: 103 us -> 72.2 us (0.70)
  Pallas kernels: 97.8 us -> 69.8 us
  local copies, waits for them, and re-layouts: 4.18 us -> 2.3 us
    pallas_call x1, Pallas kernels: 97.8 us -> 69.8 us  [per_device(): pl.pallas_call(kernel, out_shape=jax.ShapeDtypeStruct((PACKS, ROWS, queri...]
    unnamed x7 -> x1, local copies, waits for them, and re-layouts: 4.18 us -> 2.3 us
where the time goes in v2:
time: 72.2 us; the launch traced here: 72.1 us
  Pallas kernels  69.8 us (97%)
  local copies, waits for them, and re-layouts  2.3 us (3%)
    pallas_call x1, Pallas kernels, per_device(): pl.pallas_call(kernel, out_shape=jax.ShapeDtypeStruct((PACKS, ROWS, queri...  69.8 us
    unnamed x1, local copies, waits for them, and re-layouts  2.3 us

profile of v2, /device:TPU:1, one launch (start us, length us, event | category | flops | bytes accessed | tf_op | source)
XLA Modules:
  0.0 72.1 jit_solution(14767612022294014637)
XLA Ops:
  0.0 69.8 %shard_map.46 = bf16[4,64,2048]{2,1,0:T(8,128)(2,1)} custom-call(s32[1,128]{1,0:T(1,128)} %bitcast.1, s32[128,512]{1,0:T(8,128)} %seg_ref.1, bf16[4,64,2048]{2,1,0:T(8,128)(2,1)} %q_ref.1, bf16[4,64,1024]{2,1,0:T(8,128)(2,1)} %kv_ref.1), custom_call_target="tpu_custom_call" | custom-call | flops 2000000000 | bytes 4194304 | tf_op jit(solution)/shard_map/pallas_call | solution.py:279
  69.8 2.3 %copy.6 = bf16[4,64,2048]{2,1,0:T(8,128)(2,1)} copy(bf16[4,64,2048]{2,1,0:T(8,128)(2,1)} %shard_map.46) | data formatting | bytes 2097152

commit v3 on v2

--- a/solution.py
+++ b/solution.py
@@ -40,18 +40,17 @@
             bias[i, b * QB : (b + 1) * QB, (kb - first) * QB : (kb - first + 1) * QB] = jnp.where(same, 0.0, NEG)
 
 
-def attend(q_c, kvf, bias, att_c, i):
+def prepare(kvf, keys, values, i):
     kv = kvf[i].astype(jnp.float32)
     swapped = pltpu.roll(kv, HEAD, 1)
     left = lax.broadcasted_iota(jnp.int32, (PACK, LANES), 1) < HEAD
-    keys = (
-        jnp.where(left, kv, 0.0).astype(jnp.bfloat16),
-        jnp.where(left, 0.0, swapped).astype(jnp.bfloat16),
-    )
-    values = (
-        jnp.where(left, swapped, 1.0).astype(jnp.bfloat16),
-        jnp.where(left, 1.0, kv).astype(jnp.bfloat16),
-    )
+    keys[0, i] = jnp.where(left, kv, 0.0).astype(jnp.bfloat16)
+    keys[1, i] = jnp.where(left, 0.0, swapped).astype(jnp.bfloat16)
+    values[0, i] = jnp.where(left, swapped, 1.0).astype(jnp.bfloat16)
+    values[1, i] = jnp.where(left, 1.0, kv).astype(jnp.bfloat16)
+
+
+def attend(q_c, keys, values, bias, att_c, i):
     left_q = lax.broadcasted_iota(jnp.int32, (QB, LANES), 1) < HEAD
     for b in range(PACK // QB):
         lo, hi = max(0, b - 2) * QB, (b + 1) * QB
@@ -59,10 +58,10 @@
         mask = bias[i, b * QB : hi, 0 : hi - lo]
         sums = []
         for h in range(2):
-            s = lax.dot_general(q, keys[h][lo:hi], NT, preferred_element_type=jnp.float32) + mask
+            s = lax.dot_general(q, keys[h, i, lo:hi, :], NT, preferred_element_type=jnp.float32) + mask
             top = jnp.max(s, axis=1, keepdims=True)
             p = jnp.exp2((s - top) * EXP2_SCALE).astype(jnp.bfloat16)
-            sums.append(lax.dot_general(p, values[h][lo:hi], NN, preferred_element_type=jnp.float32))
+            sums.append(lax.dot_general(p, values[h, i, lo:hi, :], NN, preferred_element_type=jnp.float32))
         total = jnp.where(left_q, sums[0], sums[1])
         norm = pltpu.roll(jnp.where(left_q, sums[1], sums[0]), HEAD, 1)
         att_c[i, b * QB : hi, :] = (total / norm).astype(jnp.bfloat16)
@@ -70,7 +69,7 @@
 
 def kernel(
     plan_ref, seg_ref, q_ref, kv_ref, out_ref,
-    kvf, bias, qf0, qf1, att0, att1, mid0, mid1, snd0, snd1, segs, inv_row, inv_ref, q_v, kv_v,
+    kvf, bias, qf0, qf1, att0, att1, mid0, mid1, snd0, snd1, segs, inv_row, inv_ref, q_v, kv_v, keys, values, plan_row,
     kv_recv, q_recv, p1_send, mid_recv, mid_send, out_recv, out_send, small, group_in, all_in,
 ):
     rank, ctx = lax.axis_index("dp"), lax.axis_index("ctx")
@@ -123,6 +122,8 @@
     first = pl.multiple_of((rank >> 1) * 2 * PACKS, 2 * PACKS)
     seg_copy = pltpu.make_async_copy(seg_ref.at[pl.ds(first, 2 * PACKS)], segs, small.at[0])
     seg_copy.start()
+    plan_copy = pltpu.make_async_copy(plan_ref, plan_row, small.at[4])
+    plan_copy.start()
     own = (pltpu.make_async_copy(kv_ref, kv_v, small.at[2]), pltpu.make_async_copy(q_ref, q_v, small.at[3]))
     for copy in own:
         copy.start()
@@ -149,8 +150,8 @@
     def _():
         lax.fori_loop(0, RANKS, lambda m, _: (tell(barrier, ((rank + m) & 31, 1)), 0)[1], 0)
 
-
-    place = jnp.transpose(jnp.broadcast_to(plan_ref[...], (ALL, ALL)))
+    plan_copy.wait()
+    place = jnp.transpose(jnp.broadcast_to(plan_row[...], (ALL, ALL)))
     wanted = lax.broadcasted_iota(jnp.int32, (ALL, ALL), 1)
     source = lax.broadcasted_iota(jnp.int32, (ALL, ALL), 0)
     inv_row[...] = jnp.max(jnp.where(place == wanted, source, 0), axis=0, keepdims=True)
@@ -163,39 +164,45 @@
         pl.semaphore_wait(barrier, RANKS)
         lax.fori_loop(1, CTX, lambda m, _: (tell(all_in, (rank, (1 + m) & 7)), 0)[1], 0)
 
+    for i in range(PACKS):
+        make_bias(segs, (rank & 1) * PACKS + i, bias, i)
+
+    def far_first(k):
+        return ZN // 2 + (1 - 2 * (k & 1)) * ((k + 1) >> 1)
+
     def spread(c, i):
         dst = mid[c].at[rank * PACKS + i]
 
-        def row(m, _):
-            x = (xs + m) & 3
-            for n in range(ZN):
-                z = (zs + n) & 7
+        def ring(k, _):
+            z = (zs + far_first(k)) & 7
+            for m in range(XN):
+                x = (xs + m) & 3
                 block = ((z + ctx) & 7) * XN + x
                 src = att[c].at[i, pl.ds(pl.multiple_of(block * SUB, SUB), SUB), :]
-                if n:
+                if m:
                     remote(src, dst, mid_send.at[c], mid_recv.at[c], (x * ZN + z, ctx))
                 else:
 
-                    @pl.when(m == 0)
+                    @pl.when(z == zs)
                     def _():
                         pltpu.make_async_copy(src, dst, mid_recv.at[c]).start()
 
-                    @pl.when(m != 0)
+                    @pl.when(z != zs)
                     def _():
                         remote(src, dst, mid_send.at[c], mid_recv.at[c], (x * ZN + z, ctx))
 
             return 0
 
-        lax.fori_loop(0, XN, row, 0)
+        lax.fori_loop(0, ZN, ring, 0)
 
     for c in range(2):
 
         def work(i, _):
             if c == 0:
                 await_bytes(kvf.at[i], kv_recv.at[i])
-                make_bias(segs, (rank & 1) * PACKS + i, bias, i)
+                prepare(kvf, keys, values, i)
             await_bytes(qf[c].at[i], q_recv.at[c, i])
-            attend(qf[c], kvf, bias, att[c], i)
+            attend(qf[c], keys, values, bias, att[c], i)
             if c == 0:
 
                 @pl.when((ctx != 1) & (i == 0))
@@ -231,17 +238,17 @@
             pl.ds(pl.multiple_of(ctx * 2 * LANES + c * LANES, LANES), LANES),
         ]
 
-        def deliver(m, _):
-            for n in range(ZN):
-                to = ((xs + m) & 3) * ZN + ((zs + n) & 7)
+        def deliver(k, _):
+            z = (zs + far_first(k)) & 7
+            for m in range(XN):
+                to = ((xs + m) & 3) * ZN + z
                 for j in range(PACKS):
                     snd[c][to * PACKS + j] = mid[c][inv_ref[0, to * PACKS + j]]
                 src = snd[c].at[pl.ds(to * PACKS, PACKS)]
-                if n:
+                if m:
                     remote(src, dst, out_send.at[c], out_recv, (to, to_ctx))
                 else:
-
-                    here = (m == 0) & (zs == 0)
+                    here = (z == zs) & (zs == 0)
 
                     @pl.when(here)
                     def _():
@@ -253,7 +260,7 @@
 
             return 0
 
-        lax.fori_loop(0, XN, deliver, 0)
+        lax.fori_loop(0, ZN, deliver, 0)
 
     await_bytes(kvf.at[:, 0 : PACK - ROWS], p1_send.at[0])
     await_bytes(qf0.at[:, 0 : PACK - ROWS], p1_send.at[1])
@@ -280,10 +287,10 @@
         kernel,
         out_shape=jax.ShapeDtypeStruct((PACKS, ROWS, queries.shape[2]), jnp.bfloat16),
         in_specs=[
-            pl.BlockSpec(memory_space=pltpu.VMEM),
-            pl.BlockSpec(memory_space=pl.ANY),
-            pl.BlockSpec(memory_space=pl.ANY),
-            pl.BlockSpec(memory_space=pl.ANY),
+            pl.BlockSpec(memory_space=pltpu.HBM),
+            pl.BlockSpec(memory_space=pltpu.HBM),
+            pl.BlockSpec(memory_space=pltpu.HBM),
+            pl.BlockSpec(memory_space=pltpu.HBM),
         ],
         out_specs=pl.BlockSpec(memory_space=pl.ANY),
         scratch_shapes=[
@@ -296,6 +303,8 @@
             pltpu.SMEM((1, ALL), jnp.int32),
             pltpu.VMEM(queries.shape, jnp.bfloat16),
             pltpu.VMEM(keyvals.shape, jnp.bfloat16),
+            *[pltpu.VMEM((2, PACKS, PACK, LANES), jnp.bfloat16)] * 2,
+            pltpu.VMEM((1, ALL), jnp.int32),
             dma((PACKS,)),
             dma((2, PACKS)),
             dma((3,)),
@@ -303,13 +312,13 @@
             dma((2,)),
             dma(()),
             dma((2,)),
-            dma((4,)),
+            dma((5,)),
             pltpu.SemaphoreType.REGULAR,
             pltpu.SemaphoreType.REGULAR,
         ],
-        compiler_params=pltpu.CompilerParams(collective_id=0, has_side_effects=True, vmem_limit_bytes=60 * 2**20),
+        compiler_params=pltpu.CompilerParams(collective_id=0, has_side_effects=True, vmem_limit_bytes=24 * 2**20),
         cost_estimate=pl.CostEstimate(flops=2 * 10**9, bytes_accessed=4 * 2**20, transcendentals=2 * 10**6),
-    )(plan.reshape(1, ALL), segments, queries, keyvals)
+    )(*(pltpu.with_memory_space_constraint(a, pltpu.HBM) for a in (plan.reshape(1, ALL), segments, queries, keyvals)))
 
 
 def solution(mesh):

time: 72.2 us -> 68.4 us (0.947)
  Pallas kernels: 69.8 us -> 67.3 us
  local copies, waits for them, and re-layouts: 2.3 us -> 0.97 us
    pallas_call x1, Pallas kernels: 69.8 us -> 67.3 us  [per_device(): pl.pallas_call(kernel, out_shape=jax.ShapeDtypeStruct((PACKS, ROWS, queri...]
    unnamed x1, local copies, waits for them, and re-layouts: 2.3 us -> 0.97 us
where the time goes in v3:
time: 68.4 us; the launch traced here: 68.3 us
  Pallas kernels  67.3 us (98%)
  local copies, waits for them, and re-layouts  0.97 us (1%)
    pallas_call x1, Pallas kernels, per_device(): pl.pallas_call(kernel, out_shape=jax.ShapeDtypeStruct((PACKS, ROWS, queri...  67.3 us

profile of v3, /device:TPU:1, one launch (start us, length us, event | category | flops | bytes accessed | tf_op | source)
XLA Modules:
  0.0 68.3 jit_solution(2701126991096104572)
XLA Ops:
  0.0 67.3 %shard_map.46 = bf16[4,64,2048]{2,1,0:T(8,128)(2,1)S(1)} custom-call(s32[1,128]{1,0:T(1,128)} %bitcast.1, s32[128,512]{1,0:T(8,128)} %seg_ref.1, bf16[4,64,2048]{2,1,0:T(8,128)(2,1)} %q_ref.1, bf16[4,64,1024]{2,1,0:T(8,128)(2,1)} %kv_ref.1), custom_call_target="tpu_custom_call" | custom-call | flops 2000000000 | bytes 4194304 | tf_op jit(solution)/shard_map/pallas_call | solution.py:286
  67.3 1.0 %copy.6 = bf16[4,64,2048]{2,1,0:T(8,128)(2,1)} copy(bf16[4,64,2048]{2,1,0:T(8,128)(2,1)S(1)} %shard_map.46) | data formatting | bytes 2097152

commit v4 on v3

--- a/solution.py
+++ b/solution.py
@@ -44,27 +44,28 @@
     kv = kvf[i].astype(jnp.float32)
     swapped = pltpu.roll(kv, HEAD, 1)
     left = lax.broadcasted_iota(jnp.int32, (PACK, LANES), 1) < HEAD
-    keys[0, i] = jnp.where(left, kv, 0.0).astype(jnp.bfloat16)
-    keys[1, i] = jnp.where(left, 0.0, swapped).astype(jnp.bfloat16)
-    values[0, i] = jnp.where(left, swapped, 1.0).astype(jnp.bfloat16)
-    values[1, i] = jnp.where(left, 1.0, kv).astype(jnp.bfloat16)
+    keys[i] = jnp.where(left, kv, 0.0).astype(jnp.bfloat16)
+    values[i] = jnp.where(left, swapped, 1.0).astype(jnp.bfloat16)
 
 
 def attend(q_c, keys, values, bias, att_c, i):
-    left_q = lax.broadcasted_iota(jnp.int32, (QB, LANES), 1) < HEAD
+    left = lax.broadcasted_iota(jnp.int32, (QB, LANES), 1) < HEAD
+    left_two = lax.broadcasted_iota(jnp.int32, (2 * QB, LANES), 1) < HEAD
     for b in range(PACK // QB):
         lo, hi = max(0, b - 2) * QB, (b + 1) * QB
         q = q_c[i, b * QB : hi, :]
+        other = pltpu.roll(q.astype(jnp.float32), HEAD, 1).astype(jnp.bfloat16)
+        both = jnp.concatenate([q, other], axis=0)
+        s = lax.dot_general(both, keys[i, lo:hi, :], NT, preferred_element_type=jnp.float32)
         mask = bias[i, b * QB : hi, 0 : hi - lo]
-        sums = []
-        for h in range(2):
-            s = lax.dot_general(q, keys[h, i, lo:hi, :], NT, preferred_element_type=jnp.float32) + mask
-            top = jnp.max(s, axis=1, keepdims=True)
-            p = jnp.exp2((s - top) * EXP2_SCALE).astype(jnp.bfloat16)
-            sums.append(lax.dot_general(p, values[h, i, lo:hi, :], NN, preferred_element_type=jnp.float32))
-        total = jnp.where(left_q, sums[0], sums[1])
-        norm = pltpu.roll(jnp.where(left_q, sums[1], sums[0]), HEAD, 1)
-        att_c[i, b * QB : hi, :] = (total / norm).astype(jnp.bfloat16)
+        s = (s.reshape(2, QB, hi - lo) + mask[None]).reshape(2 * QB, hi - lo)
+        top = jnp.max(s, axis=1, keepdims=True)
+        p = jnp.exp2((s - top) * EXP2_SCALE).astype(jnp.bfloat16)
+        sums = lax.dot_general(p, values[i, lo:hi, :], NN, preferred_element_type=jnp.float32)
+        norm = jnp.where(left_two, pltpu.roll(sums, HEAD, 1), 1.0)
+        mixed = sums / norm
+        out = jnp.where(left, mixed[:QB], pltpu.roll(mixed[QB:], HEAD, 1))
+        att_c[i, b * QB : hi, :] = out.astype(jnp.bfloat16)
 
 
 def kernel(
@@ -303,7 +304,7 @@
             pltpu.SMEM((1, ALL), jnp.int32),
             pltpu.VMEM(queries.shape, jnp.bfloat16),
             pltpu.VMEM(keyvals.shape, jnp.bfloat16),
-            *[pltpu.VMEM((2, PACKS, PACK, LANES), jnp.bfloat16)] * 2,
+            *[pltpu.VMEM(full, jnp.bfloat16)] * 2,
             pltpu.VMEM((1, ALL), jnp.int32),
             dma((PACKS,)),
             dma((2, PACKS)),

time: 68.4 us -> 67.5 us (0.987)
  Pallas kernels: 67.3 us -> 66.4 us
    pallas_call x1, Pallas kernels: 67.3 us -> 66.4 us  [per_device(): pl.pallas_call(kernel, out_shape=jax.ShapeDtypeStruct((PACKS, ROWS, queri...]
where the time goes in v4:
time: 67.5 us; the launch traced here: 67.4 us
  Pallas kernels  66.4 us (98%)
  local copies, waits for them, and re-layouts  0.97 us (1%)
    pallas_call x1, Pallas kernels, per_device(): pl.pallas_call(kernel, out_shape=jax.ShapeDtypeStruct((PACKS, ROWS, queri...  66.4 us

profile of v4, /device:TPU:1, one launch (start us, length us, event | category | flops | bytes accessed | tf_op | source)
XLA Modules:
  0.0 67.4 jit_solution(12596009000515042094)
XLA Ops:
  0.0 66.4 %shard_map.46 = bf16[4,64,2048]{2,1,0:T(8,128)(2,1)S(1)} custom-call(s32[1,128]{1,0:T(1,128)} %bitcast.1, s32[128,512]{1,0:T(8,128)} %seg_ref.1, bf16[4,64,2048]{2,1,0:T(8,128)(2,1)} %q_ref.1, bf16[4,64,1024]{2,1,0:T(8,128)(2,1)} %kv_ref.1), custom_call_target="tpu_custom_call" | custom-call | flops 2000000000 | bytes 4194304 | tf_op jit(solution)/shard_map/pallas_call | solution.py:287
  66.5 1.0 %copy.6 = bf16[4,64,2048]{2,1,0:T(8,128)(2,1)} copy(bf16[4,64,2048]{2,1,0:T(8,128)(2,1)S(1)} %shard_map.46) | data formatting | bytes 2097152

commit v5 on v4

--- a/solution.py
+++ b/solution.py
@@ -50,7 +50,6 @@
 
 def attend(q_c, keys, values, bias, att_c, i):
     left = lax.broadcasted_iota(jnp.int32, (QB, LANES), 1) < HEAD
-    left_two = lax.broadcasted_iota(jnp.int32, (2 * QB, LANES), 1) < HEAD
     for b in range(PACK // QB):
         lo, hi = max(0, b - 2) * QB, (b + 1) * QB
         q = q_c[i, b * QB : hi, :]
@@ -62,9 +61,8 @@
         top = jnp.max(s, axis=1, keepdims=True)
         p = jnp.exp2((s - top) * EXP2_SCALE).astype(jnp.bfloat16)
         sums = lax.dot_general(p, values[i, lo:hi, :], NN, preferred_element_type=jnp.float32)
-        norm = jnp.where(left_two, pltpu.roll(sums, HEAD, 1), 1.0)
-        mixed = sums / norm
-        out = jnp.where(left, mixed[:QB], pltpu.roll(mixed[QB:], HEAD, 1))
+        one, two = sums[:QB], sums[QB:]
+        out = jnp.where(left, one, pltpu.roll(two, HEAD, 1)) / jnp.where(left, pltpu.roll(one, HEAD, 1), two)
         att_c[i, b * QB : hi, :] = out.astype(jnp.bfloat16)
 
 

time: 67.5 us -> 67.5 us (level)
  no operation moved by 1% of the time
where the time goes in v5:
time: 67.5 us; the launch traced here: 67.4 us
  Pallas kernels  66.4 us (98%)
  local copies, waits for them, and re-layouts  0.97 us (1%)
    pallas_call x1, Pallas kernels, per_device(): pl.pallas_call(kernel, out_shape=jax.ShapeDtypeStruct((PACKS, ROWS, queri...  66.4 us

profile of v5, /device:TPU:1, one launch (start us, length us, event | category | flops | bytes accessed | tf_op | source)
XLA Modules:
  0.0 67.4 jit_solution(11240810168916903687)
XLA Ops:
  0.0 66.4 %shard_map.46 = bf16[4,64,2048]{2,1,0:T(8,128)(2,1)S(1)} custom-call(s32[1,128]{1,0:T(1,128)} %bitcast.1, s32[128,512]{1,0:T(8,128)} %seg_ref.1, bf16[4,64,2048]{2,1,0:T(8,128)(2,1)} %q_ref.1, bf16[4,64,1024]{2,1,0:T(8,128)(2,1)} %kv_ref.1), custom_call_target="tpu_custom_call" | custom-call | flops 2000000000 | bytes 4194304 | tf_op jit(solution)/shard_map/pallas_call | solution.py:285
  66.4 1.0 %copy.6 = bf16[4,64,2048]{2,1,0:T(8,128)(2,1)} copy(bf16[4,64,2048]{2,1,0:T(8,128)(2,1)S(1)} %shard_map.46) | data formatting | bytes 2097152
